TPU v7x, 32 devices: a whole 2x2x4 slice. The times are simulated.
32 devices in a mesh: pole: 2 (over x), row: 8 (over z, y), col: 2 (over core).
Axes of the slice: x: 2, y: 2, z: 4, core: 2. Of those that a mesh axis runs over, the one named last changes fastest.
Arguments:
- ancestor_inverse: float32 [24576, 12288], P(('pole', 'row'), 'col'), parts along dimension 0, may hold values from -0.0546875 to 0.0546875
- parent_panel: float32 [24576, 256], P(('pole', 'row'), 'col'), parts along dimension 0, may hold values from -0.0546875 to 0.0546875
- child_panel: float32 [24576, 256], P(('pole', 'row'), 'col'), parts along dimension 0, may hold values from -0.0546875 to 0.0546875
- child_link: float32 [4, 128, 128], P(('pole', 'col')), parts along dimension 0, may hold values from -0.5 to 0.5
- parent_pivot_inv: float32 [4, 128, 128], P(('pole', 'col')), parts along dimension 0, may hold values from -6 to 6
- child_pivot_inv: float32 [4, 128, 128], P(('pole', 'col')), parts along dimension 0, may hold values from -6 to 6
- parent_blocks: int32 [4, 96], P('pole'), parts along dimension 0, may hold values 0 or 1
- child_blocks: int32 [4, 96], P('pole'), parts along dimension 0, may hold values 0 or 1
- tree: int32 [4], P('pole'), parts along dimension 0, may hold values from 0 to 1, as said below
Outputs:
- parent_column: float32 [24576, 256], P(('pole', 'row'), 'col'), parts along dimension 0
- parent_diag: float32 [4, 128, 128], P(('pole', 'col')), parts along dimension 0
- child_column: float32 [24576, 256], P(('pole', 'row'), 'col'), parts along dimension 0
- child_cross: float32 [4, 128, 128], P(('pole', 'col')), parts along dimension 0
- child_diag: float32 [4, 128, 128], P(('pole', 'col')), parts along dimension 0
There are 2 independent parts, one for each index of `pole`. A program takes and returns all parts, laid end to end along the dimension named above; each array names one. Nothing has to cross between parts.
Inputs may be any that keep to these rules, and one draw needn't show every extreme that they name: `tree`: each child's parent among the 2 parent supernodes; every parent has the same number of children.
All inputs are finite; a program needn't handle non-finite values.
Results may differ from a plain program's by a relative error of at most 0.000071.
Values sent between devices are 32-bit elements; how exact they have to be, the bound alone decides.
A program may use at most 192 MiB of HBM per device.

v0:
```python
import jax
import jax.numpy as jnp
from jax import lax
from jax.sharding import PartitionSpec as P

HIGH = lax.Precision.HIGHEST


def expand_mask(mask_rows, width):
    table = mask_rows.T.astype(jnp.float32)
    return jnp.repeat(jnp.repeat(table, width, axis=0), width, axis=1)


def per_device(
    ancestor_inverse,
    parent_panel,
    child_panel,
    child_link,
    parent_pivot_inv,
    child_pivot_inv,
    parent_blocks,
    child_blocks,
    tree,
):
    width = child_link.shape[1]
    local_rows = ancestor_inverse.shape[0]
    row_index = lax.axis_index("row")
    col_index = lax.axis_index("col")
    blocks_here = local_rows // width
    parents_here = parent_panel.shape[1] // width
    children_here = child_panel.shape[1] // width
    parent_count = parent_blocks.shape[0]
    block_start = row_index * blocks_here
    parent_slice = lax.dynamic_slice(
        parent_blocks, (col_index * parents_here, block_start), (parents_here, blocks_here)
    )
    parent_masked = parent_panel * expand_mask(parent_slice, width)
    tree_local = lax.dynamic_slice_in_dim(tree, col_index * children_here, children_here, 0)
    onehot = (tree_local[:, None] == jnp.arange(parent_count, dtype=jnp.int32)[None, :]).astype(
        jnp.float32
    )
    parent_rows_here = lax.dynamic_slice_in_dim(parent_blocks, block_start, blocks_here, 1).astype(
        jnp.float32
    )
    inherited = jnp.dot(
        onehot, parent_rows_here, precision=HIGH, preferred_element_type=jnp.float32
    )
    kept = lax.dynamic_slice(
        child_blocks, (col_index * children_here, block_start), (children_here, blocks_here)
    ).astype(jnp.float32)
    child_masked = child_panel * expand_mask(inherited * kept, width)
    parent_tall, child_tall = (
        lax.all_gather(parent_masked, "row", axis=0, tiled=True),
        lax.all_gather(child_masked, "row", axis=0, tiled=True),
    )
    parent_mine, child_mine = (
        lax.all_to_all(parent_tall, "col", split_axis=0, concat_axis=1, tiled=True),
        lax.all_to_all(child_tall, "col", split_axis=0, concat_axis=1, tiled=True),
    )
    joined = jnp.concatenate([parent_mine, child_mine], axis=1)
    product = jnp.dot(ancestor_inverse, joined, precision=HIGH, preferred_element_type=jnp.float32)
    split_at = parent_mine.shape[1]
    parent_sum, child_sum = (
        lax.psum_scatter(product[:, :split_at], "col", scatter_dimension=1, tiled=True),
        lax.psum_scatter(product[:, split_at:], "col", scatter_dimension=1, tiled=True),
    )
    parent_column = -parent_sum
    partial_value = jnp.einsum(
        "snw,snv->nwv",
        parent_masked.reshape(local_rows, parents_here, width),
        parent_column.reshape(local_rows, parents_here, width),
        precision=HIGH,
    )
    parent_diag = parent_pivot_inv - lax.psum(partial_value, "row")
    column_all, diag_all = (
        lax.all_gather(parent_column, "col", axis=1, tiled=True),
        lax.all_gather(parent_diag, "col", axis=0, tiled=True),
    )
    selected = jnp.einsum(
        "cp,spw->scw", onehot, column_all.reshape(local_rows, parent_count, width), precision=HIGH
    )
    parent_pick = jnp.einsum("cp,pwv->cwv", onehot, diag_all, precision=HIGH)
    child_three = child_masked.reshape(local_rows, children_here, width)
    child_col3 = -(
        child_sum.reshape(local_rows, children_here, width)
        + jnp.einsum("scw,cwv->scv", selected, child_link, precision=HIGH)
    )
    cross_part = jnp.einsum("scw,scv->cwv", selected, child_three, precision=HIGH)
    diag_part = jnp.einsum("scw,scv->cwv", child_three, child_col3, precision=HIGH)
    cross_total, diag_total = lax.psum((cross_part, diag_part), "row")
    child_cross = -(
        cross_total + jnp.einsum("cwu,cuv->cwv", parent_pick, child_link, precision=HIGH)
    )
    child_diag = (
        child_pivot_inv
        - diag_total
        - jnp.einsum("cuw,cuv->cwv", child_link, child_cross, precision=HIGH)
    )
    return (
        parent_column,
        parent_diag,
        child_col3.reshape(local_rows, children_here * width),
        child_cross,
        child_diag,
    )


def solution(mesh):
    return jax.shard_map(
        per_device,
        mesh=mesh,
        in_specs=(
            P(("pole", "row"), "col"),
            P(("pole", "row"), "col"),
            P(("pole", "row"), "col"),
            P(("pole", "col"), None, None),
            P(("pole", "col"), None, None),
            P(("pole", "col"), None, None),
            P("pole", None),
            P("pole", None),
            P("pole"),
        ),
        out_specs=(
            P(("pole", "row"), "col"),
            P(("pole", "col"), None, None),
            P(("pole", "row"), "col"),
            P(("pole", "col"), None, None),
            P(("pole", "col"), None, None),
        ),
        check_vma=False,
    )
```

profile of v0, /device:TPU:0, one launch (start us, length us, event | category | flops | bytes accessed | tf_op | source)
XLA Modules:
  0.0 425.8 jit_solution(9301198252035302032)
XLA Ops:
  7.2 1.3 dynamic_slice.13
  8.6 1.6 fusion.13
  10.2 2.3 broadcast_multiply_fusion
  12.6 0.8 convert_bitcast_fusion
  13.4 2.3 broadcast_multiply_fusion.1
  15.8 98.6 %all-gather.6.cloned.1.call-done = f32[12288,128]{1,0:T(8,128)} async-done(((f32[1536,128]{1,0:T(8,128)}), f32[12288,128]{1,0:T(8,128)}) %all-gather.6.cloned.1.call-update) | async-done | bytes 6291472 | tf_op jit(solution)/shard_map/all_gather | solution.py:54
  114.4 15.2 %all_to_all.38 = f32[2,6144,128]{2,1,0:T(8,128)} all-to-all(f32[2,6144,128]{2,1,0:T(8,128)} %bitcast.91), channel_id=1, replica_groups=mesh['pole'=2,'row'=8,'col'=2] {'col'}, dimensions={0} | all-to-all | bytes 12582912 | tf_op jit(solution)/shard_map/all_to_all | solution.py:58
  129.6 6.6 %copy.29 = f32[6144,2,128]{0,2,1:T(8,128)} copy(f32[6144,2,128]{2,0,1:T(8,128)} %bitcast.89) | data formatting | bytes 12582912 | tf_op jit(solution)/shard_map/all_to_all | solution.py:58
  136.2 78.2 %all-gather.4.cloned.1.call-done = f32[12288,128]{1,0:T(8,128)} async-done(((f32[1536,128]{1,0:T(8,128)}), f32[12288,128]{1,0:T(8,128)}) %all-gather.4.cloned.1.call-update) | async-done | bytes 6291472 | tf_op jit(solution)/shard_map/all_gather | solution.py:53
  214.4 15.2 %all_to_all.39 = f32[2,6144,128]{2,1,0:T(8,128)} all-to-all(f32[2,6144,128]{2,1,0:T(8,128)} %bitcast.92), channel_id=1, replica_groups=mesh['pole'=2,'row'=8,'col'=2] {'col'}, dimensions={0} | all-to-all | bytes 12582912 | tf_op jit(solution)/shard_map/all_to_all | solution.py:57
  229.6 6.6 %copy.28 = f32[6144,2,128]{0,2,1:T(8,128)} copy(f32[6144,2,128]{2,0,1:T(8,128)} %bitcast.90) | data formatting | bytes 12582912 | tf_op jit(solution)/shard_map/all_to_all | solution.py:57
  236.2 64.8 %fusion.4 = f32[1536,512]{0,1:T(8,128)S(1)} fusion(f32[1536,6144]{1,0:T(8,128)} %param.9, f32[6144,256]{0,1:T(8,128)} %bitcast.93, f32[6144,256]{0,1:T(8,128)} %bitcast.94), kind=kOutput, calls=%fused_computation.4 | convolution fusion | flops 57985204224 | bytes 53477376 | tf_op jit(solution)/shard_map/dot_general | solution.py:61
  301.0 1.9 fusion.34
  303.0 7.3 %reduce-scatter.3.cloned.1.call-done = f32[1536,128]{0,1:T(8,128)} async-done(((f32[1536,256]{0,1:T(8,128)}), f32[1536,128]{0,1:T(8,128)}) %reduce-scatter.3.cloned.1.call-update) | async-done | bytes 786448 | tf_op jit(solution)/shard_map/reduce_scatter | solution.py:64
  310.3 2.1 neg.9
  312.5 0.5 reduce-scatter.5.cloned.1.call-update
  313.3 3.2 convolution_bitcast_fusion.3
  316.4 7.2 %all-gather.8.cloned.1.call-done = f32[1536,256]{0,1:T(8,128)} async-done(((f32[1536,128]{0,1:T(8,128)}), f32[1536,256]{0,1:T(8,128)}) %all-gather.8.cloned.1.call-update) | async-done | bytes 1572880 | tf_op jit(solution)/shard_map/all_gather | solution.py:76
  323.6 3.6 copy.34
  327.2 5.3 %fusion.22 = f32[1,1536,128]{2,0,1:T(1,128)S(1)} fusion(f32[1536,2,128]{2,1,0:T(2,128)} %copy.34, s32[]{:T(128)} %bitcast.5), kind=kOutput, calls=%fused_computation.32 | convolution fusion | flops 4718594 | bytes 2359300 | tf_op jit(solution)/shard_map/cp,spw->scw/dot_general | solution.py:79
  332.6 2.0 convolution_bitcast_fusion.2
  334.6 1.4 reduce-scatter.5.cloned.1.call-done
  336.0 2.0 fusion.9
  338.0 2.0 convolution_bitcast_fusion.1
  340.1 1.1 copy.32
  341.3 1.1 copy.33
  342.4 69.9 %all-reduce.3.cloned.1.call-done = (f32[1,128,128]{2,1,0:T(8,128)}, f32[1,128,128]{2,1,0:T(8,128)}, f32[1,128,128]{2,1,0:T(8,128)}) async-done(((f32[1,128,128]{2,1,0:T(8,128)}, f32[1,128,128]{2,1,0:T(8,128)}, f32[1,128,128]{2,1,0:T(8,128)}), (f32[1,128,128]{2,1,0:T(8,128)}, f32[1,128,128]{2,1,0:T(8,128)}, f32[1,128,128]{2,1,0:T(8,128)})) %all-reduce.3.cloned.1.call-update) | async-done | bytes 196624 | tf_op jit(solution)/shard_map/psum | solution.py:74
  412.3 0.8 sub.9
  413.1 1.9 all_gather.15
  415.0 1.1 fusion.14
  416.1 1.0 fusion.12
  417.2 1.8 fusion.10
  (29 shorter events, 0.7 us)
Async XLA Ops:
  7.2 328.9 %copy-start = (f32[1,128,128]{2,1,0:T(8,128)S(1)}, f32[1,128,128]{2,1,0:T(8,128)}, u32[]{:S(2)}) copy-start(f32[1,128,128]{2,1,0:T(8,128)} %param.12) | copy-start | bytes 196612
  7.2 107.2 %all-gather.6.cloned.1.call-start = ((), (), s32[]{:S(2)}) async-start(), calls=%async_computation.5 | async-start | bytes 7077888 | tf_op jit(solution)/shard_map/all_gather | solution.py:54
  12.5 201.9 %all-gather.4.cloned.1.call-start = ((), (), s32[]{:S(2)}) async-start(), calls=%async_computation.4 | async-start | bytes 7077888 | tf_op jit(solution)/shard_map/all_gather | solution.py:53
  15.7 294.6 %reduce-scatter.3.cloned.1.call-start = ((), (), s32[]{:S(2)}) async-start(), calls=%async_computation.6 | async-start | bytes 2359296 | tf_op jit(solution)/shard_map/reduce_scatter | solution.py:64
  301.0 12.2 %copy-start.2 = (f32[1536,128]{1,0:T(8,128)S(1)}, f32[1536,128]{1,0:T(8,128)}, u32[]{:S(2)}) copy-start(f32[1536,128]{1,0:T(8,128)} %broadcast_multiply_fusion.1) | copy-start | bytes 2359300
  302.9 29.7 %copy-start.1 = (f32[1536,128]{1,0:T(8,128)S(1)}, f32[1536,128]{1,0:T(8,128)}, u32[]{:S(2)}) copy-start(f32[1536,128]{1,0:T(8,128)} %broadcast_multiply_fusion) | copy-start | bytes 2359300
  302.9 20.7 %all-gather.8.cloned.1.call-start = ((), (), s32[]{:S(2)}) async-start(), calls=%async_computation.8 | async-start | bytes 2359296 | tf_op jit(solution)/shard_map/all_gather | solution.py:76
  312.4 23.6 %reduce-scatter.5.cloned.1.call-start = ((), (), s32[]{:S(2)}) async-start(), calls=%async_computation.7 | async-start | bytes 2359296 | tf_op jit(solution)/shard_map/reduce_scatter | solution.py:65
  313.0 99.2 %all-reduce.3.cloned.1.call-start = ((), (), s32[]{:S(2)}) async-start(), calls=%async_computation.9 | async-start | bytes 393216 | tf_op jit(solution)/shard_map/psum | solution.py:74
  316.4 23.7 %copy-start.3 = (f32[1536,128]{0,1:T(8,128)S(1)}, f32[1536,128]{0,1:T(8,128)}, u32[]{:S(2)}) copy-start(f32[1536,128]{0,1:T(8,128)} %neg.9) | copy-start | bytes 2359300
  327.2 85.0 %copy-start.6 = (f32[1,128,128]{2,1,0:T(8,128)S(1)}, f32[1,128,128]{2,1,0:T(8,128)}, u32[]{:S(2)}) copy-start(f32[1,128,128]{2,1,0:T(8,128)} %param.13) | copy-start | bytes 196612
  327.2 90.0 %copy-start.7 = (f32[1,128,128]{2,1,0:T(8,128)S(1)}, f32[1,128,128]{2,1,0:T(8,128)}, u32[]{:S(2)}) copy-start(f32[1,128,128]{2,1,0:T(8,128)} %param.14) | copy-start | bytes 196612
  413.1 5.9 %copy-start.4 = (f32[1,128,128]{2,1,0:T(8,128)}, f32[1,128,128]{2,1,0:T(8,128)S(1)}, u32[]{:S(2)}) copy-start(f32[1,128,128]{2,1,0:T(8,128)S(1)} %sub.9) | copy-start | bytes 196612
  417.2 1.8 copy-start.5
Sparse Core Ops, SparseCore 0:
  12.6 101.7 all-gather.5
  117.2 97.2 all-gather.3
  303.0 7.2 reduce-scatter.2
  312.5 11.0 all-gather.7
  325.8 10.2 reduce-scatter.4
  340.2 71.9 all-reduce.2
where the time goes:
time: 427 us; the launch traced here: 426 us
  waiting for transfers between devices  263 us (62%)
  matrix products  84.8 us (20%)
  blocking collectives  32.3 us (8%)
  local copies, waits for them, and re-layouts  22.6 us (5%)
  between operations  14.2 us (3%)
  other arithmetic  8.28 us (2%)
    all_gather x1, waiting for transfers between devices, per_device(): lax.all_gather(child_masked, 'row', axis=0, tiled=True)  98.6 us
    all_gather x1, waiting for transfers between devices, per_device(): lax.all_gather(parent_masked, 'row', axis=0, tiled=True)  78.2 us
    psum x1, waiting for transfers between devices, per_device(): parent_diag = parent_pivot_inv - lax.psum(partial_value, 'row')  69.9 us
    dot_general x1, matrix products, per_device(): jnp.dot(ancestor_inverse, joined, precision=HIGH, preferred_element_type=...  64.8 us
    all_to_all x1, blocking collectives, per_device(): lax.all_to_all(child_tall, 'col', split_axis=0, concat_axis=1, tiled=True)  15.2 us
    all_to_all x1, blocking collectives, per_device(): lax.all_to_all(parent_tall, 'col', split_axis=0, concat_axis=1, tiled=True)  15.2 us
  transfers between devices with their start and end apart: 6, of which 6 were waited for; matrix products, arithmetic and copies ran while one was open for 6% of the time, Pallas kernels for 0%

commit v1 on v0

v1 whole, which is shorter than its diff:
```python
import functools

import jax
import jax.numpy as jnp
from jax import lax
from jax.experimental import pallas as pl
from jax.experimental.pallas import tpu as pltpu
from jax.sharding import PartitionSpec as P

HIGH = lax.Precision.HIGHEST
MESH = pl.DeviceIdType.MESH
LAG = 2


def expand_mask(mask_rows, width):
    table = mask_rows.T.astype(jnp.float32)
    return jnp.repeat(jnp.repeat(table, width, axis=0), width, axis=1)


def split(value):
    high = value.astype(jnp.bfloat16)
    return high, (value - high.astype(jnp.float32)).astype(jnp.bfloat16)


def dot_split(left, right):
    lh, ll = left
    rh, rl = right
    dot = functools.partial(jnp.dot, preferred_element_type=jnp.float32)
    return dot(lh, rh) + (dot(lh, rl) + dot(ll, rh))


def dot3(left, right):
    return dot_split(split(left), split(right))


def kernel(
    geo, tree_ref, own_ref, a_ref, link_ref, pivot_ref,
    pcol_ref, ccol_ref, part_ref, pick_ref,
    panel, acc, a_buf, halves, other, pivots,
    own_sem, sib_send, sib_recv, recv, send, a_sem, ex_send, ex_recv, pv_send, pv_recv,
):
    deep, wide, rows, piece, tile, w = geo
    half, cuts, tiles = deep // 2, rows // piece, rows // tile
    own_slot = half * wide
    count = half * cuts
    row, c = lax.axis_index("row"), lax.axis_index("col")
    z, y = row // wide, row % wide
    m = z + c * (deep - 1 - 2 * z)
    sibling = {"row": row, "col": 1 - c}

    def row_at(place, column):
        return (place + c * (deep - 1 - 2 * place)) * wide + column

    def local(source, column):
        return (source + c * (half - 1 - 2 * source)) * wide + column

    def source_of(j):
        left, right = m, half - 1 - m
        both = jnp.minimum(left, right)
        step = (j + 1) // 2
        near = m + jnp.where(j % 2 == 1, step, -step)
        far = jnp.where(left > right, m - (j - both), m + (j - both))
        inside = jnp.where(j <= 2 * both, near, far)
        return jnp.where(m >= half, half - 1 - j, inside)

    has_right, has_left = m + 1 < deep, m >= 1
    barrier = pltpu.get_barrier_semaphore()
    pl.semaphore_signal(barrier, inc=1, device_id=sibling, device_id_type=MESH)

    @pl.when(has_right)
    def _():
        pl.semaphore_signal(
            barrier, inc=1, device_id={"row": row_at(m + 1, y), "col": c}, device_id_type=MESH
        )

    @pl.when(has_left)
    def _():
        pl.semaphore_signal(
            barrier, inc=1, device_id={"row": row_at(m - 1, y), "col": c}, device_id_type=MESH
        )

    if wide == 2:
        pl.semaphore_signal(
            barrier, inc=1, device_id={"row": row_at(m, 1 - y), "col": c}, device_id_type=MESH
        )

    own_lanes = pl.ds(pl.multiple_of(c * 2 * w, 2 * w), 2 * w)

    def own_copy():
        return pltpu.make_async_copy(own_ref, panel.at[own_slot, :, own_lanes], own_sem)

    def sib_copy(q):
        at = pl.ds(pl.multiple_of(q * piece, piece), piece)
        return pltpu.make_async_remote_copy(
            src_ref=own_ref.at[at],
            dst_ref=panel.at[own_slot, at, own_lanes],
            send_sem=sib_send.at[q],
            recv_sem=sib_recv.at[q],
            device_id=sibling,
            device_id_type=MESH,
        )

    def pivot_copy():
        return pltpu.make_async_remote_copy(
            src_ref=pivot_ref,
            dst_ref=pivots,
            send_sem=pv_send,
            recv_sem=pv_recv,
            device_id=sibling,
            device_id_type=MESH,
        )

    def where_is(i, column):
        source, q = source_of(i // cuts), i % cuts
        return source, q, local(source, column)

    def a_copy(kind, i):
        column = y if kind == 0 else 1 - y
        _, q, slot = where_is(i, column)
        at = pl.ds(pl.multiple_of(slot * rows + q * piece, piece), piece)
        return pltpu.make_async_copy(
            a_ref.at[:, at], a_buf.at[kind, i % 2], a_sem.at[kind, i % 2]
        )

    def forward(way, i):
        source, q, slot = where_is(i, y)
        here = jnp.where(source == m, own_slot, slot)
        at = pl.ds(pl.multiple_of(q * piece, piece), piece)
        target = (row_at(m + 1, y), row_at(m - 1, y), row_at(m, 1 - y))[way]
        return pltpu.make_async_remote_copy(
            src_ref=panel.at[here, at],
            dst_ref=panel.at[slot, at],
            send_sem=send.at[way, i],
            recv_sem=recv.at[slot * cuts + q],
            device_id={"row": target, "col": c},
            device_id_type=MESH,
        )

    def each_forward(i, act):
        source, _, _ = where_is(i, y)

        @pl.when(has_right & (source <= m))
        def _():
            act(forward(0, i))

        @pl.when(has_left & (source >= m))
        def _():
            act(forward(1, i))

        if wide == 2:
            act(forward(2, i))

    def arrived(slot, q):
        at = pl.ds(pl.multiple_of(q * piece, piece), piece)
        pltpu.make_async_remote_copy(
            src_ref=panel.at[slot, at],
            dst_ref=panel.at[slot, at],
            send_sem=send.at[0, 0],
            recv_sem=recv.at[slot * cuts + q],
            device_id=sibling,
            device_id_type=MESH,
        ).wait_recv()

    def multiply(slot, q, kind, i):
        at = pl.ds(pl.multiple_of(q * piece, piece), piece)
        halves[0], halves[1] = split(panel[slot, at])

        def one(t, carry):
            r = pl.ds(pl.multiple_of(t * tile, tile), tile)
            left = split(a_buf[kind, i % 2, r])
            acc[r] += dot_split(left, (halves[0], halves[1]))
            return carry

        lax.fori_loop(0, tiles, one, 0)

    a_copy(0, 0).start()
    if wide == 2:
        a_copy(1, 0).start()
    own_copy().start()
    acc[...] = jnp.zeros_like(acc)
    part_ref[...] = jnp.zeros_like(part_ref)
    greeted = 1 + (wide == 2) + has_right.astype(jnp.int32) + has_left.astype(jnp.int32)
    pl.semaphore_wait(barrier, greeted)

    def start_sib(q, carry):
        sib_copy(q).start()
        return carry

    lax.fori_loop(0, cuts, start_sib, 0)
    pivot_copy().start()
    own_copy().wait()

    def step(i, carry):
        @pl.when(i < count)
        def _():
            source, q, slot = where_is(i, y)
            mine = source == m

            @pl.when(mine)
            def _():
                sib_copy(q).wait_recv()

            @pl.when(jnp.logical_not(mine))
            def _():
                arrived(slot, q)

            each_forward(i, lambda copy: copy.start())
            a_copy(0, i).wait()

            @pl.when(i + 1 < count)
            def _():
                a_copy(0, i + 1).start()

            multiply(jnp.where(mine, own_slot, slot), q, 0, i)

        if wide == 2:

            @pl.when(i >= LAG)
            def _():
                t = i - LAG
                _, q, slot = where_is(t, 1 - y)
                arrived(slot, q)
                a_copy(1, t).wait()

                @pl.when(t + 1 < count)
                def _():
                    a_copy(1, t + 1).start()

                multiply(slot, q, 1, t)

        return carry

    lax.fori_loop(0, count + (LAG if wide == 2 else 0), step, 0)

    def ex_copy(t, which):
        r = pl.ds(pl.multiple_of(t * tile, tile), tile)
        lanes = (0, 2 * w, (1 - c) * 2 * w + w)[which]
        lanes = pl.ds(pl.multiple_of(lanes, w), w)
        return pltpu.make_async_remote_copy(
            src_ref=acc.at[r, lanes],
            dst_ref=other.at[which, r],
            send_sem=ex_send.at[t, which],
            recv_sem=ex_recv.at[t, which],
            device_id=sibling,
            device_id_type=MESH,
        )

    def ex_start(t, carry):
        for which in range(3):
            ex_copy(t, which).start()
        return carry

    lax.fori_loop(0, tiles, ex_start, 0)

    @pl.when(m >= half)
    def _():
        def sib_wait(q, carry):
            sib_copy(q).wait_recv()
            return carry

        lax.fori_loop(0, cuts, sib_wait, 0)

    pick = tree_ref[c].astype(jnp.float32)
    side = c.astype(jnp.float32)

    def choose(by, first, second):
        return first * (1.0 - by) + second * by

    link = split(link_ref[0])

    def tail(t, carry):
        r = pl.ds(pl.multiple_of(t * tile, tile), tile)
        for which in range(3):
            ex_copy(t, which).wait_recv()
        p0 = -(acc[r, 0:w] + other[0, r])
        p1 = -(acc[r, 2 * w : 3 * w] + other[1, r])
        total = choose(side, acc[r, w : 2 * w], acc[r, 3 * w : 4 * w]) + other[2, r]
        chip = panel[own_slot, r]
        m0, m1 = chip[:, 0:w], chip[:, 2 * w : 3 * w]
        kids = choose(side, chip[:, w : 2 * w], chip[:, 3 * w :])
        pcol = choose(side, p0, p1)
        chosen = choose(pick, p0, p1)
        ccol = -(total + dot_split(split(chosen), link))
        pcol_ref[r] = pcol
        ccol_ref[r] = ccol
        own_t = split(choose(side, m0, m1).T)
        pick_t = split(choose(pick, m0, m1).T)
        kids_t = split(kids.T)
        part_ref[0] += dot_split(own_t, split(pcol))
        part_ref[1] += dot_split(pick_t, split(chosen))
        part_ref[2] += dot_split(split(chosen.T), split(kids))
        part_ref[3] += dot_split(kids_t, split(ccol))
        return carry

    lax.fori_loop(0, tiles, tail, 0)

    pivot_copy().wait()
    first = choose(side, pivot_ref[0], pivots[0])
    second = choose(side, pivots[0], pivot_ref[0])
    pick_ref[...] = choose(pick, first, second)

    def drain(i, carry):
        each_forward(i, lambda copy: copy.wait_send())
        return carry

    lax.fori_loop(0, count, drain, 0)

    def drain_sib(q, carry):
        sib_copy(q).wait_send()
        return carry

    lax.fori_loop(0, cuts, drain_sib, 0)

    def drain_ex(t, carry):
        for which in range(3):
            ex_copy(t, which).wait_send()
        return carry

    lax.fori_loop(0, tiles, drain_ex, 0)


def columns(wide, tree, own, ancestor_inverse, link, pivot):
    rows, w = own.shape[0], link.shape[1]
    line = lax.axis_size("row") // wide
    piece = 256 if rows % 256 == 0 else 128
    tile = piece
    half, cuts, tiles = line // 2, rows // piece, rows // piece
    count = half * cuts
    f32 = jnp.float32
    vmem = pl.BlockSpec(memory_space=pltpu.VMEM)
    anywhere = pl.BlockSpec(memory_space=pl.ANY)
    dma = pltpu.SemaphoreType.DMA
    flops = 2 * rows * ancestor_inverse.shape[1] * 4 * w * 3
    return pl.pallas_call(
        functools.partial(kernel, (line, wide, rows, piece, tile, w)),
        out_shape=(
            jax.ShapeDtypeStruct((rows, w), f32),
            jax.ShapeDtypeStruct((rows, w), f32),
            jax.ShapeDtypeStruct((4, w, w), f32),
            jax.ShapeDtypeStruct((w, w), f32),
        ),
        in_specs=[pl.BlockSpec(memory_space=pltpu.SMEM), anywhere, anywhere, vmem, vmem],
        out_specs=(vmem, vmem, vmem, vmem),
        scratch_shapes=[
            pltpu.VMEM((half * wide + 1, rows, 4 * w), f32),
            pltpu.VMEM((rows, 4 * w), f32),
            pltpu.VMEM((wide, 2, rows, piece), f32),
            pltpu.VMEM((2, piece, 4 * w), jnp.bfloat16),
            pltpu.VMEM((3, rows, w), f32),
            pltpu.VMEM((1, w, w), f32),
            dma,
            dma((cuts,)),
            dma((cuts,)),
            dma((half * wide * cuts,)),
            dma((3, count)),
            dma((wide, 2)),
            dma((tiles, 3)),
            dma((tiles, 3)),
            dma,
            dma,
        ],
        cost_estimate=pl.CostEstimate(
            flops=flops, bytes_accessed=4 * ancestor_inverse.size, transcendentals=0
        ),
        compiler_params=pltpu.CompilerParams(
            collective_id=0, has_side_effects=True, vmem_limit_bytes=48 * 2**20
        ),
    )(tree, own, ancestor_inverse, link, pivot)


def per_device(
    wide,
    ancestor_inverse,
    parent_panel,
    child_panel,
    child_link,
    parent_pivot_inv,
    child_pivot_inv,
    parent_blocks,
    child_blocks,
    tree,
):
    width = child_link.shape[1]
    rows = ancestor_inverse.shape[0]
    row_index = lax.axis_index("row")
    col_index = lax.axis_index("col")
    here = rows // width
    start = row_index * here
    parents = lax.dynamic_slice_in_dim(parent_blocks, start, here, 1)
    kept = lax.dynamic_slice(child_blocks, (col_index, start), (1, here))
    parent_mask = lax.dynamic_slice_in_dim(parents, col_index, 1, 0)
    mine = lax.dynamic_slice_in_dim(tree, col_index, 1, 0)
    inherited = jnp.where(mine[:, None] == 0, parents[0:1], parents[1:2])
    own = jnp.concatenate(
        [
            parent_panel * expand_mask(parent_mask, width),
            child_panel * expand_mask(inherited * kept, width),
        ],
        axis=1,
    )
    pcol, ccol, part, pick = columns(
        wide, tree, own, ancestor_inverse, child_link, parent_pivot_inv
    )
    total = lax.psum(part, "row")
    parent_diag = parent_pivot_inv - total[0:1]
    link = child_link[0]
    dot = functools.partial(jnp.dot, precision=HIGH, preferred_element_type=jnp.float32)
    cross = -(total[2] + dot(pick - total[1], link))
    diag = child_pivot_inv - total[3:4] - dot(link.T, cross)[None]
    return pcol, parent_diag, ccol, cross[None], diag


def solution(mesh):
    line = list(mesh.devices[0, :, 0])
    places = {getattr(device, "coords", (0, index % 2, 0))[1] for index, device in enumerate(line)}
    wide = 2 if len(places) == 2 else 1
    return jax.shard_map(
        functools.partial(per_device, wide),
        mesh=mesh,
        in_specs=(
            P(("pole", "row"), "col"),
            P(("pole", "row"), "col"),
            P(("pole", "row"), "col"),
            P(("pole", "col"), None, None),
            P(("pole", "col"), None, None),
            P(("pole", "col"), None, None),
            P("pole", None),
            P("pole", None),
            P("pole"),
        ),
        out_specs=(
            P(("pole", "row"), "col"),
            P(("pole", "col"), None, None),
            P(("pole", "row"), "col"),
            P(("pole", "col"), None, None),
            P(("pole", "col"), None, None),
        ),
        check_vma=False,
    )
```

time: 427 us -> 250 us (0.59)
  waiting for transfers between devices: 263 us -> 71.5 us
  Pallas kernels: 0 us -> 151 us
  matrix products: 84.8 us -> 2.86 us
  blocking collectives: 32.3 us -> 0 us
  local copies, waits for them, and re-layouts: 22.6 us -> 4.65 us
    all_gather x3 -> x0, waiting for transfers between devices: 184 us -> none  [the longest x1 98.6 us: per_device(): lax.all_gather(child_masked, 'row', axis=0, tiled=True)]
    pallas_call x0 -> x1, Pallas kernels: none -> 151 us  [columns(): pl.pallas_call(functools.partial(kernel, (line, wide, rows, piece, tile,...]
    dot_general x10 -> x2, matrix products: 84.8 us -> 2.86 us  [the longest x1 1.79 us: per_device(): diag = child_pivot_inv - total[3:4] - dot(link.T, cross)[None]]
    all_to_all x2 -> x0, blocking collectives: 30.4 us -> none  [the longest x1 15.2 us: per_device(): lax.all_to_all(child_tall, 'col', split_axis=0, concat_axis=1, tiled=True)]
    all_to_all x2 -> x0, local copies, waits for them, and re-layouts: 13.3 us -> none  [the longest x1 6.64 us: per_device(): lax.all_to_all(parent_tall, 'col', split_axis=0, concat_axis=1, tiled=True)]
    reduce_scatter x2 -> x0, waiting for transfers between devices: 8.74 us -> none  [the longest x1 7.35 us: per_device(): lax.psum_scatter(product[:, :split_at], 'col', scatter_dimension=1, tiled...]
  transfers between devices with their start and end apart: 6 -> 1, of which waited for: 6 -> 1; matrix products, arithmetic and copies ran while one was open for 6% -> 0% of each run, Pallas kernels for 0% -> 0%
where the time goes in v1:
time: 250 us
  Pallas kernels  151 us (60%)
  waiting for transfers between devices  71.5 us (29%)
  between operations  14.8 us (6%)
  other arithmetic  4.93 us (2%)
  local copies, waits for them, and re-layouts  4.65 us (2%)
  matrix products  2.86 us (1%)
    pallas_call x1, Pallas kernels, columns(): pl.pallas_call(functools.partial(kernel, (line, wide, rows, piece, tile,...  151 us
    psum x1, waiting for transfers between devices, per_device(): total = lax.psum(part, 'row')  71.5 us
  transfers between devices with their start and end apart: 1, of which 1 were waited for; matrix products, arithmetic and copies ran while one was open for 0% of the time, Pallas kernels for 0%

profile of v1, /device:TPU:0, one launch (start us, length us, event | category | flops | bytes accessed | tf_op | source)
XLA Modules:
  0.0 249.6 jit_solution(14227025678487125731)
XLA Ops:
  7.2 0.0 all-reduce.2.cloned.1.call-start
  7.2 1.2 dynamic_slice.13
  8.5 0.7 constant_dynamic-slice_fusion
  9.9 0.8 fusion.8
  10.6 0.1 broadcast_bitcast_fusion
  10.7 0.8 convert_bitcast_fusion
  11.5 0.1 broadcast_bitcast_fusion.1
  11.5 1.8 broadcast_multiply_fusion
  13.4 0.0 copy-start
  13.4 0.0 copy-start.1
  13.4 0.0 copy-start.2
  13.4 0.1 pad_maximum_fusion.own_ref
  13.5 0.7 copy-done
  14.2 0.0 copy-done.1
  14.3 0.0 copy-done.2
  14.3 0.0 copy-start.4
  14.3 150.9 %shard_map.128 = (f32[1536,128]{1,0:T(8,128)S(1)}, f32[1536,128]{1,0:T(8,128)S(1)}, f32[4,128,128]{2,1,0:T(8,128)}, f32[128,128]{1,0:T(8,128)S(1)}) custom-call(s32[2]{0:T(128)S(1)} %copy-done.2, f32[1536,256]{1,0:T(8,128)S(1)} %pad_maximum_fusion.own_ref, f32[1536,6144]{1,0:T(8,128)} %a_ref.1, f32[1,128,128]{2,1,0:T(8,128)S(1)} %copy-done, ...), custom_call_target="tpu_custom_call" | custom-call | flops 28991029248 | bytes 37748736 | tf_op jit(solution)/shard_map/pallas_call | solution.py:334
  165.2 0.0 all-reduce.2.cloned.1.call-update
  165.2 71.5 %all-reduce.2.cloned.1.call-done = f32[4,128,128]{2,1,0:T(8,128)} async-done(((f32[4,128,128]{2,1,0:T(8,128)}), f32[4,128,128]{2,1,0:T(8,128)}) %all-reduce.2.cloned.1.call-update) | async-done | bytes 262160 | tf_op jit(solution)/shard_map/psum | solution.py:404
  236.7 1.5 slice_subtract_fusion.1
  238.1 1.1 fusion.1
  239.2 0.0 copy-done.4
  239.2 0.0 copy-start.3
  239.2 1.8 fusion
  241.0 0.9 copy.19
  241.9 0.9 copy.20
  242.8 0.0 copy-done.3
Async XLA Ops:
  7.2 229.5 %all-reduce.2.cloned.1.call-start = ((), (), s32[]{:S(2)}) async-start(), calls=%async_computation | async-start | bytes 524288 | tf_op jit(solution)/shard_map/psum | solution.py:404
  13.4 0.8 copy-start
  13.4 0.9 copy-start.1
  13.4 0.9 copy-start.2
  14.3 225.0 %copy-start.4 = (f32[1,128,128]{2,1,0:T(8,128)S(1)}, f32[1,128,128]{2,1,0:T(8,128)}, u32[]{:S(2)}) copy-start(f32[1,128,128]{2,1,0:T(8,128)} %param.14) | copy-start | bytes 196612
  239.2 3.6 %copy-start.3 = (f32[128,128]{1,0:T(8,128)}, f32[128,128]{1,0:T(8,128)S(1)}, u32[]{:S(2)}) copy-start(f32[128,128]{1,0:T(8,128)S(1)} %fusion.1) | copy-start | bytes 196612
Sparse Core Ops, SparseCore 0:
  165.3 71.2 all-reduce.1

commit v2 on v1

v2 whole, which is shorter than its diff:
```python
import functools

import jax
import jax.numpy as jnp
from jax import lax
from jax.experimental import pallas as pl
from jax.experimental.pallas import tpu as pltpu
from jax.sharding import PartitionSpec as P

MESH = pl.DeviceIdType.MESH
LAG = 2


def split(value):
    high = value.astype(jnp.bfloat16)
    return high, (value - high.astype(jnp.float32)).astype(jnp.bfloat16)


def dot_split(left, right):
    lh, ll = left
    rh, rl = right
    dot = functools.partial(jnp.dot, preferred_element_type=jnp.float32)
    return dot(lh, rh) + (dot(lh, rl) + dot(ll, rh))


def dot3(left, right):
    return dot_split(split(left), split(right))


def kernel(
    geo, tree_ref, parents_ref, kids_ref, parent_ref, child_ref, a_ref,
    link_ref, pivot_ref, child_pivot_ref,
    pcol_ref, pdiag_ref, ccol_ref, cross_ref, cdiag_ref,
    panel, acc, a_buf, halves, other, pivots, raw, part, terms, whole,
    own_sem, sib_send, sib_recv, recv, send, a_sem, ex_send, ex_recv, pv_send, pv_recv,
    rs_send, rs_recv, ag_send, ag_recv,
):
    deep, wide, rows, piece, tile, w = geo
    line = deep * wide
    share = 4 * w // line
    half, cuts, tiles = deep // 2, rows // piece, rows // tile
    own_slot = half * wide
    count = half * cuts
    row, c = lax.axis_index("row"), lax.axis_index("col")
    z, y = row // wide, row % wide
    m = z + c * (deep - 1 - 2 * z)
    sibling = {"row": row, "col": 1 - c}

    def row_at(place, column):
        return (place + c * (deep - 1 - 2 * place)) * wide + column

    def local(source, column):
        return (source + c * (half - 1 - 2 * source)) * wide + column

    def source_of(j):
        left, right = m, half - 1 - m
        both = jnp.minimum(left, right)
        step = (j + 1) // 2
        near = m + jnp.where(j % 2 == 1, step, -step)
        far = jnp.where(left > right, m - (j - both), m + (j - both))
        inside = jnp.where(j <= 2 * both, near, far)
        return jnp.where(m >= half, half - 1 - j, inside)

    has_right, has_left = m + 1 < deep, m >= 1
    barrier = pltpu.get_barrier_semaphore()
    pl.semaphore_signal(barrier, inc=1, device_id=sibling, device_id_type=MESH)

    def greet(k, carry):
        pl.semaphore_signal(
            barrier, inc=1, device_id={"row": (row + k) % line, "col": c}, device_id_type=MESH
        )
        return carry

    lax.fori_loop(1, line, greet, 0)
    own_lanes = pl.ds(pl.multiple_of(c * 2 * w, 2 * w), 2 * w)

    def raw_copy(which):
        return pltpu.make_async_copy((parent_ref, child_ref)[which], raw.at[which], own_sem.at[which])

    def sib_copy(q):
        at = pl.ds(pl.multiple_of(q * piece, piece), piece)
        return pltpu.make_async_remote_copy(
            src_ref=panel.at[own_slot, at, own_lanes],
            dst_ref=panel.at[own_slot, at, own_lanes],
            send_sem=sib_send.at[q],
            recv_sem=sib_recv.at[q],
            device_id=sibling,
            device_id_type=MESH,
        )

    def pivot_copy():
        return pltpu.make_async_remote_copy(
            src_ref=pivot_ref,
            dst_ref=pivots,
            send_sem=pv_send,
            recv_sem=pv_recv,
            device_id=sibling,
            device_id_type=MESH,
        )

    def where_is(i, column):
        source, q = source_of(i // cuts), i % cuts
        return source, q, local(source, column)

    def a_copy(kind, i):
        column = y if kind == 0 else 1 - y
        _, q, slot = where_is(i, column)
        at = pl.ds(pl.multiple_of(slot * rows + q * piece, piece), piece)
        return pltpu.make_async_copy(
            a_ref.at[:, at], a_buf.at[kind, i % 2], a_sem.at[kind, i % 2]
        )

    def forward(way, i):
        source, q, slot = where_is(i, y)
        here = jnp.where(source == m, own_slot, slot)
        at = pl.ds(pl.multiple_of(q * piece, piece), piece)
        target = (row_at(m + 1, y), row_at(m - 1, y), row_at(m, 1 - y))[way]
        return pltpu.make_async_remote_copy(
            src_ref=panel.at[here, at],
            dst_ref=panel.at[slot, at],
            send_sem=send.at[way, i],
            recv_sem=recv.at[slot * cuts + q],
            device_id={"row": target, "col": c},
            device_id_type=MESH,
        )

    def each_forward(i, act):
        source, _, _ = where_is(i, y)

        @pl.when(has_right & (source <= m))
        def _():
            act(forward(0, i))

        @pl.when(has_left & (source >= m))
        def _():
            act(forward(1, i))

        if wide == 2:
            act(forward(2, i))

    def arrived(slot, q):
        at = pl.ds(pl.multiple_of(q * piece, piece), piece)
        pltpu.make_async_remote_copy(
            src_ref=panel.at[slot, at],
            dst_ref=panel.at[slot, at],
            send_sem=send.at[0, 0],
            recv_sem=recv.at[slot * cuts + q],
            device_id=sibling,
            device_id_type=MESH,
        ).wait_recv()

    def multiply(slot, q, kind, i, then=None):
        at = pl.ds(pl.multiple_of(q * piece, piece), piece)
        halves[0], halves[1] = split(panel[slot, at])

        def one(t, carry):
            r = pl.ds(pl.multiple_of(t * tile, tile), tile)
            left = split(a_buf[kind, i % 2, r])
            acc[r] += dot_split(left, (halves[0], halves[1]))
            if then is not None:
                then(t)
            return carry

        lax.fori_loop(0, tiles, one, 0)

    a_copy(0, 0).start()
    if wide == 2:
        a_copy(1, 0).start()
    raw_copy(0).start()
    raw_copy(1).start()
    acc[...] = jnp.zeros_like(acc)
    part[...] = jnp.zeros_like(part)
    tree = tree_ref[c]
    raw_copy(0).wait()
    raw_copy(1).wait()
    for b in range(rows // w):
        at = slice(b * w, (b + 1) * w)
        spot = row * (rows // w) + b
        inherited = parents_ref[0, spot] * (1 - tree) + parents_ref[1, spot] * tree
        keep_parent = parents_ref[c, spot].astype(jnp.float32)
        keep_child = (inherited * kids_ref[c, spot]).astype(jnp.float32)
        for core in range(2):

            @pl.when(c == core)
            def _(core=core, at=at, keep_parent=keep_parent, keep_child=keep_child):
                first = core * 2 * w
                panel[own_slot, at, first : first + w] = raw[0, at] * keep_parent
                panel[own_slot, at, first + w : first + 2 * w] = raw[1, at] * keep_child

    pl.semaphore_wait(barrier, line)

    def start_sib(q, carry):
        sib_copy(q).start()
        return carry

    lax.fori_loop(0, cuts, start_sib, 0)
    pivot_copy().start()

    def ex_copy(t, which):
        r = pl.ds(pl.multiple_of(t * tile, tile), tile)
        lanes = (0, 2 * w, (1 - c) * 2 * w + w)[which]
        lanes = pl.ds(pl.multiple_of(lanes, w), w)
        return pltpu.make_async_remote_copy(
            src_ref=acc.at[r, lanes],
            dst_ref=other.at[which, r],
            send_sem=ex_send.at[t, which],
            recv_sem=ex_recv.at[t, which],
            device_id=sibling,
            device_id_type=MESH,
        )

    def ex_start(t):
        for which in range(3):
            ex_copy(t, which).start()

    def own_step(i, then=None):
        source, q, slot = where_is(i, y)
        mine = source == m

        @pl.when(mine)
        def _():
            sib_copy(q).wait_recv()

        @pl.when(jnp.logical_not(mine))
        def _():
            arrived(slot, q)

        each_forward(i, lambda copy: copy.start())
        a_copy(0, i).wait()

        @pl.when(i + 1 < count)
        def _():
            a_copy(0, i + 1).start()

        multiply(jnp.where(mine, own_slot, slot), q, 0, i, then)

    def other_step(t, then=None):
        _, q, slot = where_is(t, 1 - y)
        arrived(slot, q)
        a_copy(1, t).wait()

        @pl.when(t + 1 < count)
        def _():
            a_copy(1, t + 1).start()

        multiply(slot, q, 1, t, then)

    def step(i, carry):
        if wide == 2:

            @pl.when(i < count)
            def _():
                own_step(i)

            @pl.when(i >= LAG)
            def _():
                other_step(i - LAG)

        else:
            own_step(i)
        return carry

    if wide == 2:
        lax.fori_loop(0, count + LAG - 1, step, 0)
        other_step(count - 1, ex_start)
    else:
        lax.fori_loop(0, count - 1, step, 0)
        own_step(count - 1, ex_start)

    @pl.when(m >= half)
    def _():
        def sib_wait(q, carry):
            sib_copy(q).wait_recv()
            return carry

        lax.fori_loop(0, cuts, sib_wait, 0)

    pick = tree.astype(jnp.float32)
    side = c.astype(jnp.float32)

    def choose(by, first, second):
        return first * (1.0 - by) + second * by

    link = split(link_ref[0])

    def tail(t, carry):
        r = pl.ds(pl.multiple_of(t * tile, tile), tile)
        for which in range(3):
            ex_copy(t, which).wait_recv()
        p0 = -(acc[r, 0:w] + other[0, r])
        p1 = -(acc[r, 2 * w : 3 * w] + other[1, r])
        total = choose(side, acc[r, w : 2 * w], acc[r, 3 * w : 4 * w]) + other[2, r]
        chip = panel[own_slot, r]
        m0, m1 = chip[:, 0:w], chip[:, 2 * w : 3 * w]
        kids = choose(side, chip[:, w : 2 * w], chip[:, 3 * w :])
        pcol = choose(side, p0, p1)
        chosen = choose(pick, p0, p1)
        ccol = -(total + dot_split(split(chosen), link))
        pcol_ref[r] = pcol
        ccol_ref[r] = ccol
        own_t = split(choose(side, m0, m1).T)
        pick_t = split(choose(pick, m0, m1).T)
        kids_t = split(kids.T)
        part[0 * w : 1 * w] += dot_split(own_t, split(pcol))
        part[1 * w : 2 * w] += dot_split(pick_t, split(chosen))
        part[2 * w : 3 * w] += dot_split(split(chosen.T), split(kids))
        part[3 * w : 4 * w] += dot_split(kids_t, split(ccol))
        return carry

    lax.fori_loop(0, tiles, tail, 0)

    def shares(place):
        return pl.ds(pl.multiple_of(place * share, share), share)

    def rs_copy(k):
        to = (row + k) % line
        return pltpu.make_async_remote_copy(
            src_ref=part.at[shares(to)],
            dst_ref=terms.at[k],
            send_sem=rs_send.at[k],
            recv_sem=rs_recv.at[k],
            device_id={"row": to, "col": c},
            device_id_type=MESH,
        )

    def ag_copy(k):
        return pltpu.make_async_remote_copy(
            src_ref=whole.at[shares(row)],
            dst_ref=whole.at[shares(row)],
            send_sem=ag_send.at[k],
            recv_sem=ag_recv.at[k],
            device_id={"row": (row + k) % line, "col": c},
            device_id_type=MESH,
        )

    def ag_arrived(k):
        start = shares((row + line - k) % line)
        pltpu.make_async_remote_copy(
            src_ref=whole.at[start],
            dst_ref=whole.at[start],
            send_sem=ag_send.at[k],
            recv_sem=ag_recv.at[k],
            device_id=sibling,
            device_id_type=MESH,
        ).wait_recv()

    def loop(body):
        def one(k, carry):
            body(k)
            return carry

        lax.fori_loop(1, line, one, 0)

    loop(lambda k: rs_copy(k).start())

    def add_term(k, total):
        rs_copy(k).wait_recv()
        return total + terms[k]

    whole[shares(row)] = lax.fori_loop(1, line, add_term, part[shares(row)])
    loop(lambda k: ag_copy(k).start())
    pivot_copy().wait()
    first = choose(side, pivot_ref[0], pivots[0])
    second = choose(side, pivots[0], pivot_ref[0])
    chosen_pivot = choose(pick, first, second)
    loop(ag_arrived)
    pdiag_ref[0] = pivot_ref[0] - whole[0:w]
    cross = -(whole[2 * w : 3 * w] + dot_split(split(chosen_pivot - whole[w : 2 * w]), link))
    cross_ref[0] = cross
    cdiag_ref[0] = child_pivot_ref[0] - whole[3 * w :] - dot3(link_ref[0].T, cross)
    loop(lambda k: rs_copy(k).wait_send())
    loop(lambda k: ag_copy(k).wait_send())

    def drain(i, carry):
        each_forward(i, lambda copy: copy.wait_send())
        return carry

    lax.fori_loop(0, count, drain, 0)

    def drain_sib(q, carry):
        sib_copy(q).wait_send()
        return carry

    lax.fori_loop(0, cuts, drain_sib, 0)

    def drain_ex(t, carry):
        for which in range(3):
            ex_copy(t, which).wait_send()
        return carry

    lax.fori_loop(0, tiles, drain_ex, 0)


def per_device(
    wide,
    ancestor_inverse,
    parent_panel,
    child_panel,
    child_link,
    parent_pivot_inv,
    child_pivot_inv,
    parent_blocks,
    child_blocks,
    tree,
):
    rows, w = ancestor_inverse.shape[0], child_link.shape[1]
    whole_line = lax.axis_size("row")
    line = whole_line // wide
    piece = 256 if rows % 256 == 0 else 128
    tile = piece
    half, cuts, tiles = line // 2, rows // piece, rows // piece
    count = half * cuts
    f32 = jnp.float32
    scalars = pl.BlockSpec(memory_space=pltpu.SMEM)
    vmem = pl.BlockSpec(memory_space=pltpu.VMEM)
    anywhere = pl.BlockSpec(memory_space=pl.ANY)
    dma = pltpu.SemaphoreType.DMA
    flops = 2 * rows * ancestor_inverse.shape[1] * 4 * w * 3
    return pl.pallas_call(
        functools.partial(kernel, (line, wide, rows, piece, tile, w)),
        out_shape=(
            jax.ShapeDtypeStruct((rows, w), f32),
            jax.ShapeDtypeStruct((1, w, w), f32),
            jax.ShapeDtypeStruct((rows, w), f32),
            jax.ShapeDtypeStruct((1, w, w), f32),
            jax.ShapeDtypeStruct((1, w, w), f32),
        ),
        in_specs=[scalars] * 3 + [anywhere] * 3 + [vmem] * 3,
        out_specs=(vmem,) * 5,
        scratch_shapes=[
            pltpu.VMEM((half * wide + 1, rows, 4 * w), f32),
            pltpu.VMEM((rows, 4 * w), f32),
            pltpu.VMEM((wide, 2, rows, piece), f32),
            pltpu.VMEM((2, piece, 4 * w), jnp.bfloat16),
            pltpu.VMEM((3, rows, w), f32),
            pltpu.VMEM((1, w, w), f32),
            pltpu.VMEM((2, rows, w), f32),
            pltpu.VMEM((4 * w, w), f32),
            pltpu.VMEM((whole_line, 4 * w // whole_line, w), f32),
            pltpu.VMEM((4 * w, w), f32),
            dma((2,)),
            dma((cuts,)),
            dma((cuts,)),
            dma((half * wide * cuts,)),
            dma((3, count)),
            dma((wide, 2)),
            dma((tiles, 3)),
            dma((tiles, 3)),
            dma,
            dma,
            dma((whole_line,)),
            dma((whole_line,)),
            dma((whole_line,)),
            dma((whole_line,)),
        ],
        cost_estimate=pl.CostEstimate(
            flops=flops, bytes_accessed=4 * ancestor_inverse.size, transcendentals=0
        ),
        compiler_params=pltpu.CompilerParams(
            collective_id=0, has_side_effects=True, vmem_limit_bytes=48 * 2**20
        ),
    )(
        tree,
        parent_blocks,
        child_blocks,
        parent_panel,
        child_panel,
        ancestor_inverse,
        child_link,
        parent_pivot_inv,
        child_pivot_inv,
    )


def solution(mesh):
    line = list(mesh.devices[0, :, 0])
    places = {getattr(device, "coords", (0, index % 2, 0))[1] for index, device in enumerate(line)}
    wide = 2 if len(places) == 2 else 1
    return jax.shard_map(
        functools.partial(per_device, wide),
        mesh=mesh,
        in_specs=(
            P(("pole", "row"), "col"),
            P(("pole", "row"), "col"),
            P(("pole", "row"), "col"),
            P(("pole", "col"), None, None),
            P(("pole", "col"), None, None),
            P(("pole", "col"), None, None),
            P("pole", None),
            P("pole", None),
            P("pole"),
        ),
        out_specs=(
            P(("pole", "row"), "col"),
            P(("pole", "col"), None, None),
            P(("pole", "row"), "col"),
            P(("pole", "col"), None, None),
            P(("pole", "col"), None, None),
        ),
        check_vma=False,
    )
```

time: 250 us -> 176 us (0.70)
  waiting for transfers between devices: 71.5 us -> 0 us
  between operations: 14.8 us -> 0.66 us
  Pallas kernels: 151 us -> 164 us
  local copies, waits for them, and re-layouts: 4.65 us -> 10.4 us
  other arithmetic: 4.93 us -> 0 us
  matrix products: 2.86 us -> 0 us
    psum x1 -> x0, waiting for transfers between devices: 71.5 us -> none  [per_device(): total = lax.psum(part, 'row')]
    pallas_call x1, Pallas kernels: 151 us -> 164 us  [per_device(): pl.pallas_call(functools.partial(kernel, (line, wide, rows, piece, tile,...]
    unnamed x12 -> x21, local copies, waits for them, and re-layouts: 2.51 us -> 10.4 us
    dot_general x2 -> x0, matrix products: 2.86 us -> none  [the longest x1 1.79 us: per_device(): diag = child_pivot_inv - total[3:4] - dot(link.T, cross)[None]]
  transfers between devices with their start and end apart: 1 -> 0, of which waited for: 1 -> 0; matrix products, arithmetic and copies ran while one was open for 0% -> 0% of each run, Pallas kernels for 0% -> 0%
where the time goes in v2:
time: 176 us; the launch traced here: 175 us
  Pallas kernels  164 us (93%)
  local copies, waits for them, and re-layouts  10.4 us (6%)
    pallas_call x1, Pallas kernels, per_device(): pl.pallas_call(functools.partial(kernel, (line, wide, rows, piece, tile,...  164 us
    unnamed x21, local copies, waits for them, and re-layouts  10.4 us

profile of v2, /device:TPU:0, one launch (start us, length us, event | category | flops | bytes accessed | tf_op | source)
XLA Modules:
  0.0 175.3 jit_solution(14805999905849337998)
XLA Ops:
  0.6 0.0 copy-start
  0.6 1.1 copy-done
  1.8 0.0 copy-start.1
  1.8 1.1 copy-done.1
  2.9 0.0 copy-start.2
  2.9 0.8 copy-done.2
  3.7 0.0 copy-start.3
  3.7 0.8 copy-done.3
  4.6 0.0 copy-start.4
  4.6 0.8 copy-done.4
  5.4 0.0 copy-start.5
  5.4 0.7 copy-done.5
  6.1 0.0 copy-start.6
  6.1 0.7 copy-done.6
  6.8 0.0 copy-start.7
  6.8 0.7 copy-done.7
  7.4 164.2 %shard_map.128 = (f32[1536,128]{1,0:T(8,128)S(1)}, f32[1,128,128]{2,1,0:T(8,128)S(1)}, f32[1536,128]{1,0:T(8,128)S(1)}, f32[1,128,128]{2,1,0:T(8,128)S(1)}, f32[1,128,128]{2,1,0:T(8,128)S(1)}) custom-call(s32[2]{0:T(128)S(1)} %copy-done.7, s32[2,96]{1,0:T(2,128)S(1)} %copy-done.5, s32[2,96]{1,0:T(2,128)S(1)} %copy-done.6, f32[1536,128]{1,0:T(8,128)S(1)} %copy-done, ...), custom_call_target="tpu_custom_call" | custom-call | flops 28991029248 | bytes 37748736 | tf_op jit(solution)/shard_map/pallas_call | solution.py:419
  171.6 0.9 copy.19
  172.5 0.6 copy.20
  173.2 0.9 copy.21
  174.0 0.6 copy.22
  174.7 0.6 copy.23
Async XLA Ops:
  0.6 1.1 copy-start
  1.8 1.1 copy-start.1
  2.9 0.8 copy-start.2
  3.7 0.8 copy-start.3
  4.6 0.8 copy-start.4
  5.4 0.7 copy-start.5
  6.1 0.7 copy-start.6
  6.8 0.7 copy-start.7

commit v3 on v2

v3 whole, which is shorter than its diff:
```python
import functools

import jax
import jax.numpy as jnp
from jax import lax
from jax.experimental import pallas as pl
from jax.experimental.pallas import tpu as pltpu
from jax.sharding import PartitionSpec as P

MESH = pl.DeviceIdType.MESH
LAG = 4


def split(value):
    high = value.astype(jnp.bfloat16)
    return high, (value - high.astype(jnp.float32)).astype(jnp.bfloat16)


def dot_split(left, right):
    lh, ll = left
    rh, rl = right
    dot = functools.partial(jnp.dot, preferred_element_type=jnp.float32)
    return dot(lh, rh) + (dot(lh, rl) + dot(ll, rh))


def dot3(left, right):
    return dot_split(split(left), split(right))


class RowSum:
    def __init__(self, line, share, part, terms, whole, sems):
        self.line, self.share, self.part, self.terms, self.whole = line, share, part, terms, whole
        self.sems = sems
        self.owners = part.shape[0] // share
        self.row, self.c = lax.axis_index("row"), lax.axis_index("col")

    def at(self, place):
        return pl.ds(pl.multiple_of(place * self.share, self.share), self.share)

    def copy(self, k, stage, src, dst):
        return pltpu.make_async_remote_copy(
            src_ref=src,
            dst_ref=dst,
            send_sem=self.sems.at[2 * stage, k],
            recv_sem=self.sems.at[2 * stage + 1, k],
            device_id={"row": (self.row + k) % self.line, "col": self.c},
            device_id_type=MESH,
        )

    def scatter(self, k):
        to = (self.row + k) % self.line
        return self.copy(k, 0, self.part.at[self.at(to)], self.terms.at[k])

    def gather(self, k):
        return self.copy(k, 1, self.whole.at[self.at(self.row)], self.whole.at[self.at(self.row)])

    def guard(self, place, act):
        if self.owners == self.line:
            act()
        else:
            pl.when(place < self.owners)(act)

    def loop(self, body):
        def one(k, carry):
            body(k)
            return carry

        lax.fori_loop(1, self.line, one, 0)

    def start(self):
        self.loop(
            lambda k: self.guard((self.row + k) % self.line, lambda: self.scatter(k).start())
        )

    def reduce(self):
        def act():
            def add_term(k, total):
                self.scatter(k).wait_recv()
                return total + self.terms[k]

            mine = self.at(self.row)
            self.whole[mine] = lax.fori_loop(1, self.line, add_term, self.part[mine])
            self.loop(lambda k: self.gather(k).start())

        self.guard(self.row, act)

    def finish(self):
        def one(k):
            origin = (self.row + self.line - k) % self.line
            spot = self.whole.at[self.at(origin)]
            self.guard(origin, lambda: self.copy(k, 1, spot, spot).wait_recv())

        self.loop(one)

    def drain(self):
        self.loop(
            lambda k: self.guard((self.row + k) % self.line, lambda: self.scatter(k).wait_send())
        )
        self.guard(self.row, lambda: self.loop(lambda k: self.gather(k).wait_send()))


def kernel(
    geo, tree_hbm, parents_hbm, kids_hbm, parent_ref, child_ref, a_ref,
    link_ref, pivot_ref, child_pivot_ref,
    pcol_ref, pdiag_ref, ccol_ref, cross_ref, cdiag_ref,
    tree_ref, parents_ref, kids_ref,
    panel, acc, a_buf, halves, other0, other1, raw, const, diags,
    part0, terms0, whole0, part1, terms1, whole1,
    in_sem, sib_send, sib_recv, recv, send, send_more, a_sem, ex_send, ex_recv, pd_sem,
    sems0, sems1,
):
    deep, wide, rows, piece, tile, w = geo
    line = deep * wide
    half, cuts, tiles = deep // 2, rows // piece, rows // tile
    own_slot = half * wide
    per = half * cuts
    count = 2 * per
    lag = LAG if wide == 2 else 0
    row, c = lax.axis_index("row"), lax.axis_index("col")
    z, y = row // wide, row % wide
    m = z + c * (deep - 1 - 2 * z)
    sibling = {"row": row, "col": 1 - c}
    sum0 = RowSum(line, 2 * w // line, part0, terms0, whole0, sems0)
    sum1 = RowSum(line, max(8, w // line), part1, terms1, whole1, sems1)

    def row_at(place, column):
        return (place + c * (deep - 1 - 2 * place)) * wide + column

    def local(source, column):
        return (source + c * (half - 1 - 2 * source)) * wide + column

    def source_of(j):
        left, right = m, half - 1 - m
        both = jnp.minimum(left, right)
        step = (j + 1) // 2
        near = m + jnp.where(j % 2 == 1, step, -step)
        far = jnp.where(left > right, m - (j - both), m + (j - both))
        inside = jnp.where(j <= 2 * both, near, far)
        return jnp.where(m >= half, half - 1 - j, inside)

    def cut(q):
        return pl.ds(pl.multiple_of(q * piece, piece), piece)

    def tile_at(t):
        return pl.ds(pl.multiple_of(t * tile, tile), tile)

    has_right, has_left = m + 1 < deep, m >= 1
    barrier = pltpu.get_barrier_semaphore()
    pl.semaphore_signal(barrier, inc=1, device_id=sibling, device_id_type=MESH)

    def greet(k, carry):
        pl.semaphore_signal(
            barrier, inc=1, device_id={"row": (row + k) % line, "col": c}, device_id_type=MESH
        )
        return carry

    lax.fori_loop(1, line, greet, 0)

    own_lanes = pl.ds(pl.multiple_of(c * w, w), w)

    def sib_copy(n):
        phase, at = n // cuts, cut(n % cuts)
        return pltpu.make_async_remote_copy(
            src_ref=raw.at[phase, at],
            dst_ref=panel.at[phase, own_slot, at, own_lanes],
            send_sem=sib_send.at[n],
            recv_sem=sib_recv.at[n],
            device_id=sibling,
            device_id_type=MESH,
        )

    def pd_copy():
        return pltpu.make_async_remote_copy(
            src_ref=diags.at[0],
            dst_ref=diags.at[1],
            send_sem=pd_sem.at[0],
            recv_sem=pd_sem.at[1],
            device_id=sibling,
            device_id_type=MESH,
        )

    def where_is(i, column):
        phase, rest = i // per, i % per
        source, q = source_of(rest // cuts), rest % cuts
        return phase, source, q, local(source, column)

    def flag(phase, slot, q):
        return (phase * half * wide + slot) * cuts + q

    def a_copy(kind, i):
        column = y if kind == 0 else 1 - y
        _, _, q, slot = where_is(i, column)
        at = pl.ds(pl.multiple_of(slot * rows + q * piece, piece), piece)
        return pltpu.make_async_copy(
            a_ref.at[:, at], a_buf.at[kind, i % 2], a_sem.at[kind, i % 2]
        )

    def hop(way, i, kind):
        column = y if kind == 0 else 1 - y
        phase, source, q, slot = where_is(i, column)
        here = jnp.where(source == m, own_slot, slot) if kind == 0 else slot
        target = (row_at(m + 1, y), row_at(m - 1, y), row_at(m, 1 - y))[way]
        return pltpu.make_async_remote_copy(
            src_ref=panel.at[phase, here, cut(q)],
            dst_ref=panel.at[phase, slot, cut(q)],
            send_sem=(send if kind == 0 else send_more).at[way, i],
            recv_sem=recv.at[flag(phase, slot, q)],
            device_id={"row": target, "col": c},
            device_id_type=MESH,
        )

    def each_hop(i, kind, act):
        _, source, q, _ = where_is(i, y)
        around = q == cuts - 1
        along = around if kind == 1 else True

        @pl.when(has_right & (source <= m) & along)
        def _():
            act(hop(0, i, kind))

        @pl.when(has_left & (source >= m) & along)
        def _():
            act(hop(1, i, kind))

        if wide == 2 and kind == 0:

            @pl.when(jnp.logical_not(around) | (source == m))
            def _():
                act(hop(2, i, kind))

    def arrived(phase, slot, q):
        spot = panel.at[phase, slot, cut(q)]
        pltpu.make_async_remote_copy(
            src_ref=spot,
            dst_ref=spot,
            send_sem=send.at[0, 0],
            recv_sem=recv.at[flag(phase, slot, q)],
            device_id=sibling,
            device_id_type=MESH,
        ).wait_recv()

    def ex_copy(phase, t):
        r = tile_at(t)
        if phase == 0:
            src, dst = acc.at[0, r], other0.at[r]
        else:
            lanes = pl.ds(pl.multiple_of((1 - c) * w, w), w)
            src, dst = acc.at[1, r, lanes], other1.at[r]
        return pltpu.make_async_remote_copy(
            src_ref=src,
            dst_ref=dst,
            send_sem=ex_send.at[phase, t],
            recv_sem=ex_recv.at[phase, t],
            device_id=sibling,
            device_id_type=MESH,
        )

    def multiply(phase, slot, q, kind, i, closes):
        halves[0], halves[1] = split(panel[phase, slot, cut(q)])

        def one(t, carry):
            r = tile_at(t)
            left = split(a_buf[kind, i % 2, r])
            acc[phase, r] += dot_split(left, (halves[0], halves[1]))
            if closes:

                @pl.when(i == per - 1)
                def _():
                    ex_copy(0, t).start()

                @pl.when(i == count - 1)
                def _():
                    ex_copy(1, t).start()

            return carry

        lax.fori_loop(0, tiles, one, 0)

    inputs = (
        (tree_hbm, tree_ref),
        (parents_hbm, parents_ref),
        (kids_hbm, kids_ref),
        (parent_ref, raw.at[0]),
        (child_ref, raw.at[1]),
        (link_ref.at[0], const.at[0]),
        (pivot_ref.at[0], const.at[1]),
        (child_pivot_ref.at[0], const.at[2]),
    )
    loads = [
        pltpu.make_async_copy(src, dst, in_sem.at[n]) for n, (src, dst) in enumerate(inputs)
    ]
    for load in loads:
        load.start()
    a_copy(0, 0).start()
    if wide == 2:
        a_copy(1, 0).start()
    for load in loads:
        load.wait()
    tree = tree_ref[c]
    for b in range(rows // w):
        at = slice(b * w, (b + 1) * w)
        spot = row * (rows // w) + b
        inherited = parents_ref[0, spot] * (1 - tree) + parents_ref[1, spot] * tree
        raw[0, at] = raw[0, at] * parents_ref[c, spot].astype(jnp.float32)
        raw[1, at] = raw[1, at] * (inherited * kids_ref[c, spot]).astype(jnp.float32)
    pl.semaphore_wait(barrier, line)

    def start_sib(n, carry):
        sib_copy(n).start()
        return carry

    lax.fori_loop(0, 2 * cuts, start_sib, 0)
    for core in range(2):

        @pl.when(c == core)
        def _(core=core):
            for phase in range(2):
                panel[phase, own_slot, :, core * w : (core + 1) * w] = raw[phase]

    acc[...] = jnp.zeros_like(acc)
    part0[...] = jnp.zeros_like(part0)
    part1[...] = jnp.zeros_like(part1)

    pick = tree.astype(jnp.float32)
    side = c.astype(jnp.float32)

    def choose(by, first, second):
        return first * (1.0 - by) + second * by

    def own_step(i):
        phase, source, q, slot = where_is(i, y)
        mine = source == m

        @pl.when(mine)
        def _():
            sib_copy(phase * cuts + q).wait_recv()

        @pl.when(jnp.logical_not(mine))
        def _():
            arrived(phase, slot, q)

        each_hop(i, 0, lambda copy: copy.start())
        a_copy(0, i).wait()

        @pl.when(i + 1 < count)
        def _():
            a_copy(0, i + 1).start()

        multiply(phase, jnp.where(mine, own_slot, slot), q, 0, i, wide == 1)

    def other_step(i):
        phase, _, q, slot = where_is(i, 1 - y)
        arrived(phase, slot, q)
        each_hop(i, 1, lambda copy: copy.start())
        a_copy(1, i).wait()

        @pl.when(i + 1 < count)
        def _():
            a_copy(1, i + 1).start()

        multiply(phase, slot, q, 1, i, True)

    def parents_done():
        link = split(const[0])

        def one(t, carry):
            r = tile_at(t)
            ex_copy(0, t).wait_recv()
            both = -(acc[0, r] + other0[r])
            p0, p1 = both[:, :w], both[:, w:]
            pcol, chosen = choose(side, p0, p1), choose(pick, p0, p1)
            pcol_ref[r] = pcol
            ccol_ref[r] = -dot_split(split(chosen), link)
            part0[:w] += dot_split(split(raw[0, r].T), split(pcol))
            part0[w:] += dot_split(split(chosen.T), split(raw[1, r]))
            return carry

        lax.fori_loop(0, tiles, one, 0)
        sum0.start()

    def diag_done():
        sum0.finish()
        diag = const[1] - whole0[:w]
        diags[0] = diag
        pdiag_ref[0] = diag
        pd_copy().start()

    def step(i, carry):
        if wide == 2:

            @pl.when(i < count)
            def _():
                own_step(i)

            @pl.when(i >= lag)
            def _():
                other_step(i - lag)

        else:
            own_step(i)
        done = i - lag
        pl.when(done == per + per // 6 - 1)(parents_done)
        pl.when(done == per + per // 2 - 1)(sum0.reduce)
        pl.when(done == per + 5 * per // 6 - 1)(diag_done)
        return carry

    lax.fori_loop(0, count + lag, step, 0)

    def children_done(t, carry):
        r = tile_at(t)
        ex_copy(1, t).wait_recv()
        total = choose(side, acc[1, r, :w], acc[1, r, w:]) + other1[r]
        ccol = ccol_ref[r] - total
        ccol_ref[r] = ccol
        part1[...] += dot_split(split(raw[1, r].T), split(ccol))
        return carry

    lax.fori_loop(0, tiles, children_done, 0)
    sum1.start()
    pd_copy().wait()
    first = choose(side, diags[0], diags[1])
    second = choose(side, diags[1], diags[0])
    cross = -(whole0[w:] + dot3(choose(pick, first, second), const[0]))
    cross_ref[0] = cross
    cdiag_ref[0] = const[2] - dot3(const[0].T, cross)
    sum1.reduce()

    @pl.when(m >= half)
    def _():
        def sib_wait(n, carry):
            sib_copy(n).wait_recv()
            return carry

        lax.fori_loop(0, 2 * cuts, sib_wait, 0)

    def drain(i, carry):
        each_hop(i, 0, lambda copy: copy.wait_send())
        if wide == 2:
            each_hop(i, 1, lambda copy: copy.wait_send())
        return carry

    lax.fori_loop(0, count, drain, 0)

    def drain_sib(n, carry):
        sib_copy(n).wait_send()
        return carry

    lax.fori_loop(0, 2 * cuts, drain_sib, 0)

    def drain_ex(t, carry):
        ex_copy(0, t).wait_send()
        ex_copy(1, t).wait_send()
        return carry

    lax.fori_loop(0, tiles, drain_ex, 0)
    sum1.finish()
    cdiag_ref[0] = cdiag_ref[0] - whole1[...]
    sum0.drain()
    sum1.drain()


def per_device(
    wide,
    ancestor_inverse,
    parent_panel,
    child_panel,
    child_link,
    parent_pivot_inv,
    child_pivot_inv,
    parent_blocks,
    child_blocks,
    tree,
):
    rows, w = ancestor_inverse.shape[0], child_link.shape[1]
    line = lax.axis_size("row")
    deep = line // wide
    piece = 256 if rows % 256 == 0 else 128
    tile = piece
    half, cuts, tiles = deep // 2, rows // piece, rows // tile
    count = 2 * half * cuts
    share0, share1 = 2 * w // line, max(8, w // line)
    f32 = jnp.float32
    vmem = pl.BlockSpec(memory_space=pltpu.VMEM)
    dma = pltpu.SemaphoreType.DMA
    flops = 2 * rows * ancestor_inverse.shape[1] * 4 * w * 3
    return pl.pallas_call(
        functools.partial(kernel, (deep, wide, rows, piece, tile, w)),
        out_shape=(
            jax.ShapeDtypeStruct((rows, w), f32),
            jax.ShapeDtypeStruct((1, w, w), f32),
            jax.ShapeDtypeStruct((rows, w), f32),
            jax.ShapeDtypeStruct((1, w, w), f32),
            jax.ShapeDtypeStruct((1, w, w), f32),
        ),
        in_specs=[pl.BlockSpec(memory_space=pl.ANY)] * 9,
        out_specs=(vmem,) * 5,
        scratch_shapes=[
            pltpu.SMEM(tree.shape, jnp.int32),
            pltpu.SMEM(parent_blocks.shape, jnp.int32),
            pltpu.SMEM(child_blocks.shape, jnp.int32),
            pltpu.VMEM((2, half * wide + 1, rows, 2 * w), f32),
            pltpu.VMEM((2, rows, 2 * w), f32),
            pltpu.VMEM((wide, 2, rows, piece), f32),
            pltpu.VMEM((2, piece, 2 * w), jnp.bfloat16),
            pltpu.VMEM((rows, 2 * w), f32),
            pltpu.VMEM((rows, w), f32),
            pltpu.VMEM((2, rows, w), f32),
            pltpu.VMEM((3, w, w), f32),
            pltpu.VMEM((2, w, w), f32),
            pltpu.VMEM((2 * w, w), f32),
            pltpu.VMEM((line, share0, w), f32),
            pltpu.VMEM((2 * w, w), f32),
            pltpu.VMEM((w, w), f32),
            pltpu.VMEM((line, share1, w), f32),
            pltpu.VMEM((w, w), f32),
            dma((8,)),
            dma((2 * cuts,)),
            dma((2 * cuts,)),
            dma((2 * half * wide * cuts,)),
            dma((3, count)),
            dma((2, count)),
            dma((wide, 2)),
            dma((2, tiles)),
            dma((2, tiles)),
            dma((2,)),
            dma((4, line)),
            dma((4, line)),
        ],
        cost_estimate=pl.CostEstimate(
            flops=flops, bytes_accessed=8 * ancestor_inverse.size, transcendentals=0
        ),
        compiler_params=pltpu.CompilerParams(
            collective_id=0, has_side_effects=True, vmem_limit_bytes=56 * 2**20
        ),
    )(
        tree,
        parent_blocks,
        child_blocks,
        parent_panel,
        child_panel,
        ancestor_inverse,
        child_link,
        parent_pivot_inv,
        child_pivot_inv,
    )


def solution(mesh):
    line = list(mesh.devices[0, :, 0])
    places = {getattr(device, "coords", (0, index % 2, 0))[1] for index, device in enumerate(line)}
    wide = 2 if len(places) == 2 else 1
    return jax.shard_map(
        functools.partial(per_device, wide),
        mesh=mesh,
        in_specs=(
            P(("pole", "row"), "col"),
            P(("pole", "row"), "col"),
            P(("pole", "row"), "col"),
            P(("pole", "col"), None, None),
            P(("pole", "col"), None, None),
            P(("pole", "col"), None, None),
            P("pole", None),
            P("pole", None),
            P("pole"),
        ),
        out_specs=(
            P(("pole", "row"), "col"),
            P(("pole", "col"), None, None),
            P(("pole", "row"), "col"),
            P(("pole", "col"), None, None),
            P(("pole", "col"), None, None),
        ),
        check_vma=False,
    )
```

time: 176 us -> 166 us (0.943)
  Pallas kernels: 164 us -> 157 us
  local copies, waits for them, and re-layouts: 10.4 us -> 8.54 us
    pallas_call x1, Pallas kernels: 164 us -> 157 us  [per_device(): pl.pallas_call(functools.partial(kernel, (deep, wide, rows, piece, tile,...]
    unnamed x21 -> x5, local copies, waits for them, and re-layouts: 10.4 us -> 8.54 us
where the time goes in v3:
time: 166 us
  Pallas kernels  157 us (95%)
  local copies, waits for them, and re-layouts  8.54 us (5%)
    pallas_call x1, Pallas kernels, per_device(): pl.pallas_call(functools.partial(kernel, (deep, wide, rows, piece, tile,...  157 us
    unnamed x5, local copies, waits for them, and re-layouts  8.54 us

profile of v3, /device:TPU:0, one launch (start us, length us, event | category | flops | bytes accessed | tf_op | source)
XLA Modules:
  0.0 165.7 jit_solution(2151659050316330491)
XLA Ops:
  0.6 156.6 %shard_map.128 = (f32[1536,128]{1,0:T(8,128)}, f32[1,128,128]{2,1,0:T(8,128)}, f32[1536,128]{1,0:T(8,128)}, f32[1,128,128]{2,1,0:T(8,128)}, f32[1,128,128]{2,1,0:T(8,128)}) custom-call(s32[2]{0:T(128)} %tree_hbm.1, s32[2,96]{1,0:T(2,128)} %parents_hbm.1, s32[2,96]{1,0:T(2,128)} %kids_hbm.1, f32[1536,128]{1,0:T(8,128)} %parent_ref.1, f32[1536,128]{1,0:T(8,128)} %child_ref.1, ...), custom_call_target="tpu_custom_call" | custom-call | flops 28991029248 | bytes 75497472 | tf_op jit(solution)/shard_map/pallas_call | solution.py:486
  157.2 2.1 %copy.19 = f32[1536,128]{1,0:T(8,128)} copy(f32[1536,128]{1,0:T(8,128)} %get-tuple-element.10) | data formatting | bytes 1572864
  159.3 1.5 copy.20
  160.7 2.1 %copy.21 = f32[1536,128]{1,0:T(8,128)} copy(f32[1536,128]{1,0:T(8,128)} %get-tuple-element.12) | data formatting | bytes 1572864
  162.8 1.5 copy.22
  164.3 1.5 copy.23

commit v4 on v3

--- a/solution.py
+++ b/solution.py
@@ -8,7 +8,7 @@
 from jax.sharding import PartitionSpec as P
 
 MESH = pl.DeviceIdType.MESH
-LAG = 4
+LAG = 2
 
 
 def split(value):
@@ -211,7 +211,7 @@
 
     def each_hop(i, kind, act):
         _, source, q, _ = where_is(i, y)
-        around = q == cuts - 1
+        around = q == cuts // 2
         along = around if kind == 1 else True
 
         @pl.when(has_right & (source <= m) & along)
@@ -274,7 +274,7 @@
 
             return carry
 
-        lax.fori_loop(0, tiles, one, 0)
+        lax.fori_loop(0, tiles, one, 0, unroll=True)
 
     inputs = (
         (tree_hbm, tree_ref),
@@ -294,6 +294,9 @@
     a_copy(0, 0).start()
     if wide == 2:
         a_copy(1, 0).start()
+    acc[...] = jnp.zeros_like(acc)
+    part0[...] = jnp.zeros_like(part0)
+    part1[...] = jnp.zeros_like(part1)
     for load in loads:
         load.wait()
     tree = tree_ref[c]
@@ -317,9 +320,6 @@
             for phase in range(2):
                 panel[phase, own_slot, :, core * w : (core + 1) * w] = raw[phase]
 
-    acc[...] = jnp.zeros_like(acc)
-    part0[...] = jnp.zeros_like(part0)
-    part1[...] = jnp.zeros_like(part1)
 
     pick = tree.astype(jnp.float32)
     side = c.astype(jnp.float32)
@@ -375,7 +375,7 @@
             part0[w:] += dot_split(split(chosen.T), split(raw[1, r]))
             return carry
 
-        lax.fori_loop(0, tiles, one, 0)
+        lax.fori_loop(0, tiles, one, 0, unroll=True)
         sum0.start()
 
     def diag_done():
@@ -415,7 +415,7 @@
         part1[...] += dot_split(split(raw[1, r].T), split(ccol))
         return carry
 
-    lax.fori_loop(0, tiles, children_done, 0)
+    lax.fori_loop(0, tiles, children_done, 0, unroll=True)
     sum1.start()
     pd_copy().wait()
     first = choose(side, diags[0], diags[1])
@@ -457,6 +457,33 @@
     cdiag_ref[0] = cdiag_ref[0] - whole1[...]
     sum0.drain()
     sum1.drain()
+
+
+def hand_on(arrays):
+    n = len(arrays)
+
+    def body(*refs):
+        sources, targets, held, sems = refs[:n], refs[n : 2 * n], refs[2 * n : 3 * n], refs[3 * n]
+        for load in range(2):
+            pairs = zip(sources, held) if load == 0 else zip(held, targets)
+            copies = [
+                pltpu.make_async_copy(source, target, sems.at[load, k])
+                for k, (source, target) in enumerate(pairs)
+            ]
+            for copy in copies:
+                copy.start()
+            for copy in copies:
+                copy.wait()
+
+    anywhere = pl.BlockSpec(memory_space=pl.ANY)
+    return pl.pallas_call(
+        body,
+        out_shape=tuple(jax.ShapeDtypeStruct(a.shape, a.dtype) for a in arrays),
+        in_specs=[anywhere] * n,
+        out_specs=(anywhere,) * n,
+        scratch_shapes=[pltpu.VMEM(a.shape, a.dtype) for a in arrays]
+        + [pltpu.SemaphoreType.DMA((2, n))],
+    )(*arrays)
 
 
 def per_device(
@@ -483,7 +510,7 @@
     vmem = pl.BlockSpec(memory_space=pltpu.VMEM)
     dma = pltpu.SemaphoreType.DMA
     flops = 2 * rows * ancestor_inverse.shape[1] * 4 * w * 3
-    return pl.pallas_call(
+    results = pl.pallas_call(
         functools.partial(kernel, (deep, wide, rows, piece, tile, w)),
         out_shape=(
             jax.ShapeDtypeStruct((rows, w), f32),
@@ -543,6 +570,7 @@
         parent_pivot_inv,
         child_pivot_inv,
     )
+    return hand_on(results)
 
 
 def solution(mesh):

time: 166 us -> 159 us (0.958)
  local copies, waits for them, and re-layouts: 8.54 us -> 0 us
    unnamed x5 -> x0, local copies, waits for them, and re-layouts: 8.54 us -> none
    pallas_call x0 -> x1, Pallas kernels: none -> 2.67 us  [hand_on(): pl.pallas_call(body, out_shape=tuple((jax.ShapeDtypeStruct(a.shape, a.dty...]
where the time goes in v4:
time: 159 us
  Pallas kernels  158 us (99%)
    pallas_call x1, Pallas kernels, per_device(): pl.pallas_call(functools.partial(kernel, (deep, wide, rows, piece, tile,...  156 us

profile of v4, /device:TPU:0, one launch (start us, length us, event | category | flops | bytes accessed | tf_op | source)
XLA Modules:
  0.0 158.9 jit_solution(9274618083459061479)
XLA Ops:
  0.6 155.6 %shard_map.128 = (f32[1536,128]{1,0:T(8,128)}, f32[1,128,128]{2,1,0:T(8,128)}, f32[1536,128]{1,0:T(8,128)}, f32[1,128,128]{2,1,0:T(8,128)}, f32[1,128,128]{2,1,0:T(8,128)}) custom-call(s32[2]{0:T(128)} %tree_hbm.1, s32[2,96]{1,0:T(2,128)} %parents_hbm.1, s32[2,96]{1,0:T(2,128)} %kids_hbm.1, f32[1536,128]{1,0:T(8,128)} %parent_ref.1, f32[1536,128]{1,0:T(8,128)} %child_ref.1, ...), custom_call_target="tpu_custom_call" | custom-call | flops 28991029248 | bytes 75497472 | tf_op jit(solution)/shard_map/pallas_call | solution.py:513
  156.3 2.7 %shard_map.129 = (f32[1536,128]{1,0:T(8,128)}, f32[1,128,128]{2,1,0:T(8,128)}, f32[1536,128]{1,0:T(8,128)}, f32[1,128,128]{2,1,0:T(8,128)}, f32[1,128,128]{2,1,0:T(8,128)}) custom-call(f32[1536,128]{1,0:T(8,128)} %get-tuple-element.10.refs_0_, f32[1,128,128]{2,1,0:T(8,128)} %get-tuple-element.11.refs_1_, f32[1536,128]{1,0:T(8,128)} %get-tuple-element.12.refs_2_, ...), custom_call_target="tpu_custom_call" | custom-call | tf_op jit(solution)/shard_map/pallas_call | solution.py:479
